TPU v7x, 32 devices: a whole 2x2x4 slice. The times are simulated.
32 devices in a mesh: cell: 8 (over y, x, core), band: 4 (over z).
Axes of the slice: x: 2, y: 2, z: 4, core: 2. Of those that a mesh axis runs over, the one named last changes fastest.
Arguments:
- waves: float32 [192, 9464], P('band', 'cell'), may hold values from -6 to 6
- cell_matrix: float32 [32, 343, 343], P('cell')
- node_map: int32 [32, 343], P('cell'), may hold values from 0 to 1182, as said below
- share_list: int32 [8, 2, 169], P('cell'), may hold values from 0 to 1182, as said below
- contacts: int32 [2, 128], P(None, 'cell'), may hold values from 0 to 31, as said below
- proj_values: float32 [128, 8, 343], P('cell'), may hold values from -0.3125 to 0.3125
- coupling: float32 [32, 8], replicated, may hold values from -1 to 1
- proj_count: int32 [32], replicated, may hold values from 1 to 8
- mass: float32 [9464], P('cell'), may hold values from 0.5 to 2
Outputs:
- filtered: float32 [192, 9464], P('band', 'cell')
- gram: float32 [192, 192], P('band')
Inputs may be any that keep to these rules, and one draw needn't show every extreme that they name: `node_map`: row c holds local node numbers of partition c // 4; the nodes of a cell are distinct and every local node belongs to some cell of its partition. `share_list`: row 0 of partition q lists its local nodes that are also nodes of partition q - 1, row 1 those that are also nodes of partition q + 1, cyclically; the k-th node of row 1 of q is the same node as the k-th node of row 0 of q + 1. Within a partition the two rows are disjoint and their entries distinct. `contacts`: column e belongs to partition e // 16: row 0 is a local cell number below 4, row 1 an atom; no pair of cell and atom repeats within a partition. Each partition is home to 4 atoms, and every entry of an atom lies in its home partition or in one of the two beside it, cyclically.
All inputs are finite; a program needn't handle non-finite values.
Results may differ from a plain program's by a relative error of at most 0.0003.
Values may be sent and summed in bfloat16 or wider, within the bound.
A program may use at most 64 MiB of HBM per device.

v0:
```python
import math

import jax
import jax.numpy as jnp
from jax import lax
from jax.sharding import PartitionSpec as P

PRECISE = lax.Precision.HIGHEST
CENTER = 1.0
HALF_WIDTH = 1.0
LOWEST = -0.5


def extended(block, sides, width):
    for axis, dim in sides:
        count = lax.axis_size(axis)
        forward = [(i, i + 1) for i in range(count - 1)]
        forward.append((count - 1, 0))
        backward = [(target, source) for source, target in forward]
        low = lax.ppermute(
            lax.slice_in_dim(block, block.shape[dim] - width, None, axis=dim), axis, forward
        )
        high = lax.ppermute(lax.slice_in_dim(block, 0, width, axis=dim), axis, backward)
        block = jnp.concatenate([low, block, high], axis=dim)
    return block


def filter_terms():
    sigma_now = HALF_WIDTH / (LOWEST - CENTER)
    gamma_ratio = 2.0 / sigma_now
    first_scale = sigma_now / HALF_WIDTH
    later_terms = []
    for turn_index in range(2):
        sigma_next = 1.0 / (gamma_ratio - sigma_now)
        later_terms.append((2.0 * sigma_next / HALF_WIDTH, sigma_now * sigma_next))
        sigma_now = sigma_next
    return (first_scale, later_terms)


def coeff_rim(stacked):
    return extended(stacked, (("cell", 0),), 1)


def atom_rim(stacked):
    return extended(stacked, (("cell", 0),), 1)


def reach_two(single, rim_fn):
    first = rim_fn(single[None])
    second = rim_fn(jnp.stack([first[2], first[0]]))
    return jnp.concatenate([first, second[0:1], second[3:4]], axis=0)


def operate(
    values,
    cell_matrix,
    node_map,
    share_pair,
    over_cell,
    onehot_atom,
    onehot_cell,
    proj_values,
    scales,
    near_onehot,
):
    cell_vals = values[:, node_map]
    cell_out = jnp.einsum("bcj,cij->bci", cell_vals, cell_matrix, precision=PRECISE)
    entry_vals = cell_vals[:, over_cell, :]
    coeffs = jnp.einsum("bei,epi->bep", entry_vals, proj_values, precision=PRECISE)
    near_coeffs = reach_two(coeffs, coeff_rim)
    table = jnp.einsum("kbep,kea->bap", near_coeffs, near_onehot, precision=PRECISE)
    scaled = table * scales[None]
    returned = jnp.einsum("bap,ea->bep", scaled, onehot_atom, precision=PRECISE)
    added_terms = jnp.einsum("bep,epi->bei", returned, proj_values, precision=PRECISE)
    cell_out = cell_out + jnp.einsum("bei,ec->bci", added_terms, onehot_cell, precision=PRECISE)
    assembled = jnp.zeros_like(values).at[:, node_map].add(cell_out)
    face_vals = jnp.stack([assembled[:, share_pair[0]], assembled[:, share_pair[1]]])
    padded = extended(face_vals, (("cell", 0),), 1)
    return assembled.at[:, share_pair[0]].add(padded[0]).at[:, share_pair[1]].add(padded[3])


def on_device(
    waves, cell_matrix, node_map, share_list, contacts, proj_values, coupling, proj_count, mass
):
    share_pair = share_list[0]
    over_cell = contacts[0]
    atom_count, proj_slots = coupling.shape
    atom_ids = jnp.arange(atom_count, dtype=jnp.int32)
    onehot_atom = (contacts[1][:, None] == atom_ids[None, :]).astype(jnp.float32)
    onehot_cell = (
        over_cell[:, None] == jnp.arange(cell_matrix.shape[0], dtype=jnp.int32)[None, :]
    ).astype(jnp.float32)
    levels = jnp.arange(proj_slots, dtype=jnp.int32)
    scales = coupling * (levels[None, :] < proj_count[:, None]).astype(jnp.float32)
    near_atoms = reach_two(contacts[1], atom_rim)
    near_onehot = (near_atoms[:, :, None] == atom_ids[None, None, :]).astype(jnp.float32)

    def apply_operator(values):
        return operate(
            values,
            cell_matrix,
            node_map,
            share_pair,
            over_cell,
            onehot_atom,
            onehot_cell,
            proj_values,
            scales,
            near_onehot,
        )

    first_scale, later_terms = filter_terms()
    previous = waves
    current = first_scale * (apply_operator(previous) - CENTER * previous)
    for lead_scale, back_scale in later_terms:
        upcoming = lead_scale * (apply_operator(current) - CENTER * current) - back_scale * previous
        previous, current = (current, upcoming)
    node_count = waves.shape[1]
    owned = jnp.ones((node_count,), jnp.float32).at[share_pair[0]].set(0.0)
    zed = (current * (owned * jnp.sqrt(mass))[None, :]).astype(jnp.bfloat16)
    band_rows = zed.shape[0]
    groups = lax.axis_size("band")
    my_group = lax.axis_index("band")
    contract = (((1,), (1,)), ((), ()))
    column_block = lax.dot_general(
        zed,
        lax.all_gather(zed, "band", axis=0, tiled=True),
        contract,
        preferred_element_type=jnp.float32,
    )
    gram = lax.psum(column_block, "cell") / math.sqrt(lax.axis_size("cell") * node_count)
    row_ids = my_group * band_rows + jnp.arange(band_rows, dtype=jnp.int32)
    column_ids = jnp.arange(band_rows * groups, dtype=jnp.int32)
    gram = jnp.where(row_ids[:, None] == column_ids[None, :], 0.0, gram)
    return (current, gram)


def solution(mesh):
    return jax.shard_map(
        on_device,
        mesh=mesh,
        in_specs=(
            P("band", "cell"),
            P("cell", None, None),
            P("cell", None),
            P("cell", None, None),
            P(None, "cell"),
            P("cell", None, None),
            P(),
            P(),
            P("cell"),
        ),
        out_specs=(P("band", "cell"), P("band", None)),
        check_vma=False,
    )
```

profile of v0, /device:TPU:0, one launch (start us, length us, event | category | flops | bytes accessed | tf_op | source)
XLA Modules:
  0.0 234.5 jit_solution(9012266096025196245)
XLA Ops:
  2.8 3.7 %gather_fusion = f32[1372,48]{1,0:T(8,128)} fusion(f32[48,1183]{0,1:T(8,128)S(1)} %copy.82, s32[2048]{0:T(1024)S(1)} %pad_clamp_fusion), kind=kCustom, calls=%fused_computation | custom fusion | bytes 532336 | tf_op jit(solution)/shard_map/gather | solution.py:66
  9.8 2.7 %fusion.42 = f32[1,48,16,8]{1,3,2,0:T(8,128)S(1)} fusion(f32[16,8,343]{2,1,0:T(8,128)S(1)} %copy-done.1, f32[16,48,343]{2,1,0:T(8,128)} %gather_fusion.1), kind=kOutput, calls=%fused_computation.58 | convolution fusion | flops 25288704 | bytes 1253888 | tf_op jit(solution)/shard_map/bei,epi->bep/dot_general | solution.py:69
  12.9 2.9 %collective-permute-start.5 = (f32[1,48,16,8]{1,3,2,0:T(8,128)S(1)}, f32[1,48,16,8]{1,3,2,0:T(8,128)S(1)}, u32[]{:S(2)}, u32[]{:S(2)}) collective-permute-start(f32[1,48,16,8]{1,3,2,0:T(8,128)S(1)} %fusion.42), channel_id=1, source_target_pairs={{4,0},{8,4},{12,8},{16,12},{20,16},{24,20},{28,24},{0,28},{5,1},{9... | collective-permute-start | bytes 73736 | tf_op jit(solution)/shard_map/ppermute | solution.py:23
  15.9 2.6 %collective-permute-start.1 = (s32[1,16]{1,0:T(1,128)S(1)}, s32[1,16]{1,0:T(1,128)S(1)}, u32[]{:S(2)}, u32[]{:S(2)}) collective-permute-start(s32[1,16]{1,0:T(1,128)S(1)} %get-tuple-element.16), channel_id=1, source_target_pairs={{4,0},{8,4},{12,8},{16,12},{20,16},{24,20},{28,24},{0,28},{5,1},{9... | collective-permute-start | bytes 200 | tf_op jit(solution)/shard_map/ppermute | solution.py:23
  19.9 2.6 %collective-permute-start.3 = (s32[1,16]{1,0:T(1,128)S(1)}, s32[1,16]{1,0:T(1,128)S(1)}, u32[]{:S(2)}, u32[]{:S(2)}) collective-permute-start(s32[1,16]{1,0:T(1,128)S(1)} %collective-permute-done.1), channel_id=1, source_target_pairs={{4,0},{8,4},{12,8},{16,12},{20,16},{24,20},{28,24},{0,28},{5,1},{9... | collective-permute-start | bytes 200 | tf_op jit(solution)/shard_map/ppermute | solution.py:23
  23.9 2.6 %collective-permute-start.7 = (f32[1,48,16,8]{1,3,2,0:T(8,128)S(1)}, f32[1,48,16,8]{1,3,2,0:T(8,128)S(1)}, u32[]{:S(2)}, u32[]{:S(2)}) collective-permute-start(f32[1,48,16,8]{1,3,2,0:T(8,128)S(1)} %collective-permute-done.5), channel_id=1, source_target_pairs={{4,0},{8,4},{12,8},{16,12},{20,16},{24,20},{28,24},{0,28},{5,1},{9... | collective-permute-start | bytes 73736 | tf_op jit(solution)/shard_map/ppermute | solution.py:23
  31.2 2.8 %fusion.21 = f32[4,343,48]{1,2,0:T(8,128)} fusion(f32[4,343,343]{2,0,1:T(4,128)S(1)} %copy-done, f32[4,48,343]{2,0,1:T(4,128)S(1)} %fusion.16, f32[4,343,48]{1,0,2:T(4,128)S(1)} %reshape.107), kind=kOutput, calls=%fused_computation.44 | convolution fusion | flops 271129152 | bytes 2672656 | tf_op jit(solution)/shard_map/bcj,cij->bci/dot_general | solution.py:67
  38.1 9.3 %scatter_custom_fusion = f32[48,1183]{0,1:T(8,128)S(1)} fusion(s32[1372]{0:T(1024)S(1)} %reshape.248, f32[1372,48]{1,0:T(8,128)} %reshape.296, f32[]{:T(128)} %constant.13.clone.1), kind=kCustom, calls=%fused_computation.75 | custom fusion | flops 65856 | bytes 227648 | tf_op jit(solution)/shard_map/scatter-add | solution.py:76
  59.0 4.7 %gather_fusion.4 = f32[1372,48]{1,0:T(8,128)} fusion(f32[48,1183]{0,1:T(8,128)} %broadcast_multiply_fusion, s32[2048]{0:T(1024)S(1)} %pad_clamp_fusion), kind=kCustom, calls=%fused_computation.4 | custom fusion | bytes 532336 | tf_op jit(solution)/shard_map/gather | solution.py:66
  69.3 2.7 %gather_fusion.5 = f32[16,48,343]{2,1,0:T(8,128)} fusion(f32[48,4,343]{2,0,1:T(8,128)} %bitcast.180, s32[1024]{0:T(1024)} %copy-done.11), kind=kCustom, calls=%fused_computation.5 | custom fusion | bytes 2107456 | tf_op jit(solution)/shard_map/gather | solution.py:68
  72.1 2.6 %fusion.45 = f32[1,48,16,8]{1,3,2,0:T(8,128)S(1)} fusion(f32[16,8,343]{2,1,0:T(8,128)S(1)} %copy-done.1, f32[16,48,343]{2,1,0:T(8,128)} %gather_fusion.5), kind=kOutput, calls=%fused_computation.59 | convolution fusion | flops 25288704 | bytes 1253888 | tf_op jit(solution)/shard_map/bei,epi->bep/dot_general | solution.py:69
  77.4 2.6 %collective-permute-done.10 = f32[1,48,16,8]{1,3,2,0:T(8,128)S(1)} collective-permute-done((f32[1,48,16,8]{1,3,2,0:T(8,128)S(1)}, f32[1,48,16,8]{1,3,2,0:T(8,128)S(1)}, u32[]{:S(2)}, u32[]{:S(2)}) %collective-permute-start.10) | collective-permute-done | bytes 24608 | tf_op jit(solution)/shard_map/ppermute | solution.py:20
  80.0 2.6 %collective-permute-start.13 = (f32[1,48,16,8]{1,3,2,0:T(8,128)S(1)}, f32[1,48,16,8]{1,3,2,0:T(8,128)S(1)}, u32[]{:S(2)}, u32[]{:S(2)}) collective-permute-start(f32[1,48,16,8]{1,3,2,0:T(8,128)S(1)} %collective-permute-done.11), channel_id=1, source_target_pairs={{4,0},{8,4},{12,8},{16,12},{20,16},{24,20},{28,24},{0,28},{5,1},{9... | collective-permute-start | bytes 73736 | tf_op jit(solution)/shard_map/ppermute | solution.py:23
  87.2 2.8 %fusion.27 = f32[4,343,48]{1,2,0:T(8,128)} fusion(f32[4,343,343]{2,0,1:T(4,128)S(1)} %copy-done, f32[4,48,343]{2,0,1:T(4,128)S(1)} %fusion.14, f32[4,343,48]{1,0,2:T(4,128)S(1)} %copy-done.3), kind=kOutput, calls=%fused_computation.46 | convolution fusion | flops 271129152 | bytes 2672656 | tf_op jit(solution)/shard_map/bcj,cij->bci/dot_general | solution.py:67
  94.1 10.0 %scatter_custom_fusion.3 = f32[48,1183]{0,1:T(8,128)} fusion(s32[1372]{0:T(1024)S(1)} %reshape.248, f32[1372,48]{1,0:T(8,128)} %reshape.297, f32[]{:T(128)} %constant.13.clone.1), kind=kCustom, calls=%fused_computation.73 | custom fusion | flops 65856 | bytes 227648 | tf_op jit(solution)/shard_map/scatter-add | solution.py:76
  108.7 2.6 %collective-permute-start.15 = (f32[1,48,169]{1,2,0:T(8,128)}, f32[1,48,169]{1,2,0:T(8,128)}, u32[]{:S(2)}, u32[]{:S(2)}) collective-permute-start(f32[1,48,169]{1,2,0:T(8,128)} %bitcast.181), channel_id=1, source_target_pairs={{4,0},{8,4},{12,8},{16,12},{20,16},{24,20},{28,24},{0,28},{5,1},{9... | collective-permute-start | bytes 97352 | tf_op jit(solution)/shard_map/ppermute | solution.py:23
  114.2 3.6 %scatter_custom_fusion.4 = f32[48,1183]{0,1:T(8,128)} fusion(f32[48,1183]{0,1:T(8,128)} %scatter_custom_fusion.3, s32[169]{0:T(256)} %bitcast.193, f32[1,48,169]{1,2,0:T(8,128)} %collective-permute-done.14), kind=kCustom, calls=%fused_computation.86 | custom fusion | flops 8112 | bytes 317248 | tf_op jit(solution)/shard_map/scatter-add | solution.py:79
  117.8 3.6 %scatter_custom_fusion.5 = f32[48,1183]{0,1:T(8,128)} fusion(f32[48,1183]{0,1:T(8,128)} %scatter_custom_fusion.4, s32[169]{0:T(256)} %bitcast.188, f32[1,48,169]{1,2,0:T(8,128)} %collective-permute-done.15), kind=kCustom, calls=%fused_computation.84 | custom fusion | flops 8112 | bytes 317248 | tf_op jit(solution)/shard_map/scatter-add | solution.py:79
  123.5 4.7 %gather_fusion.8 = f32[1372,48]{1,0:T(8,128)} fusion(f32[48,1183]{0,1:T(8,128)} %multiply_subtract_fusion.1, s32[2048]{0:T(1024)S(1)} %pad_clamp_fusion), kind=kCustom, calls=%fused_computation.8 | custom fusion | bytes 532336 | tf_op jit(solution)/shard_map/gather | solution.py:66
  133.9 2.7 %gather_fusion.9 = f32[16,48,343]{2,1,0:T(8,128)} fusion(f32[48,4,343]{2,0,1:T(8,128)} %bitcast.179, s32[1024]{0:T(1024)} %copy-done.11), kind=kCustom, calls=%fused_computation.9 | custom fusion | bytes 2107456 | tf_op jit(solution)/shard_map/gather | solution.py:68
  136.6 3.3 %fusion.48 = f32[1,48,16,8]{1,3,2,0:T(8,128)} fusion(f32[16,8,343]{2,1,0:T(8,128)S(1)} %copy-done.1, f32[16,48,343]{2,1,0:T(8,128)} %gather_fusion.9), kind=kOutput, calls=%fused_computation.60 | convolution fusion | flops 25288704 | bytes 1253888 | tf_op jit(solution)/shard_map/bei,epi->bep/dot_general | solution.py:69
  139.9 2.7 %collective-permute-start.17 = (f32[1,48,16,8]{1,3,2,0:T(8,128)}, f32[1,48,16,8]{1,3,2,0:T(8,128)S(1)}, u32[]{:S(2)}, u32[]{:S(2)}) collective-permute-start(f32[1,48,16,8]{1,3,2,0:T(8,128)} %fusion.48), channel_id=1, source_target_pairs={{4,0},{8,4},{12,8},{16,12},{20,16},{24,20},{28,24},{0,28},{5,1},{9... | collective-permute-start | bytes 73736 | tf_op jit(solution)/shard_map/ppermute | solution.py:23
  146.5 2.6 %collective-permute-start.19 = (f32[1,48,16,8]{1,3,2,0:T(8,128)S(1)}, f32[1,48,16,8]{1,3,2,0:T(8,128)S(1)}, u32[]{:S(2)}, u32[]{:S(2)}) collective-permute-start(f32[1,48,16,8]{1,3,2,0:T(8,128)S(1)} %collective-permute-done.17), channel_id=1, source_target_pairs={{4,0},{8,4},{12,8},{16,12},{20,16},{24,20},{28,24},{0,28},{5,1},{9... | collective-permute-start | bytes 73736 | tf_op jit(solution)/shard_map/ppermute | solution.py:23
  154.6 2.8 %fusion.33 = f32[4,343,48]{1,2,0:T(8,128)} fusion(f32[4,343,343]{2,0,1:T(4,128)S(1)} %copy-done, f32[4,48,343]{2,0,1:T(4,128)S(1)} %fusion.12, f32[4,343,48]{1,0,2:T(4,128)S(1)} %copy-done.2), kind=kOutput, calls=%fused_computation.48 | convolution fusion | flops 271129152 | bytes 2672656 | tf_op jit(solution)/shard_map/bcj,cij->bci/dot_general | solution.py:67
  161.4 10.0 %scatter_custom_fusion.6 = f32[48,1183]{0,1:T(8,128)} fusion(s32[1372]{0:T(1024)S(1)} %reshape.248, f32[1372,48]{1,0:T(8,128)} %reshape.298, f32[]{:T(128)} %constant.13.clone.1), kind=kCustom, calls=%fused_computation.71 | custom fusion | flops 65856 | bytes 227648 | tf_op jit(solution)/shard_map/scatter-add | solution.py:76
  171.4 2.5 %gather_fusion.10 = f32[169,48]{1,0:T(8,128)} fusion(f32[48,1183]{0,1:T(8,128)} %scatter_custom_fusion.6, s32[1024]{0:T(1024)} %copy-done.5), kind=kCustom, calls=%fused_computation.10 | custom fusion | bytes 65572 | tf_op jit(solution)/shard_map/gather | solution.py:77
  176.2 2.6 %collective-permute-start.21 = (f32[1,48,169]{1,2,0:T(8,128)}, f32[1,48,169]{1,2,0:T(8,128)S(1)}, u32[]{:S(2)}, u32[]{:S(2)}) collective-permute-start(f32[1,48,169]{1,2,0:T(8,128)} %bitcast.182), channel_id=1, source_target_pairs={{4,0},{8,4},{12,8},{16,12},{20,16},{24,20},{28,24},{0,28},{5,1},{9... | collective-permute-start | bytes 97352 | tf_op jit(solution)/shard_map/ppermute | solution.py:23
  178.9 3.0 %collective-permute-done.20 = f32[1,48,169]{1,2,0:T(8,128)S(1)} collective-permute-done((f32[1,48,169]{1,2,0:T(8,128)}, f32[1,48,169]{1,2,0:T(8,128)S(1)}, u32[]{:S(2)}, u32[]{:S(2)}) %collective-permute-start.20) | collective-permute-done | bytes 32480 | tf_op jit(solution)/shard_map/ppermute | solution.py:20
  181.9 3.4 %scatter_custom_fusion.7 = f32[48,1183]{0,1:T(8,128)} fusion(f32[48,1183]{0,1:T(8,128)} %scatter_custom_fusion.6, s32[169]{0:T(256)} %bitcast.194, f32[1,48,169]{1,2,0:T(8,128)S(1)} %collective-permute-done.20), kind=kCustom, calls=%fused_computation.82 | custom fusion | flops 8112 | bytes 259584 | tf_op jit(solution)/shard_map/scatter-add | solution.py:79
  185.3 3.4 %scatter_custom_fusion.8 = f32[48,1183]{0,1:T(8,128)} fusion(f32[48,1183]{0,1:T(8,128)} %scatter_custom_fusion.7, s32[169]{0:T(256)} %bitcast.189, f32[1,48,169]{1,2,0:T(8,128)S(1)} %collective-permute-done.21), kind=kCustom, calls=%fused_computation.80 | custom fusion | flops 8112 | bytes 259584 | tf_op jit(solution)/shard_map/scatter-add | solution.py:79
  192.3 16.7 %all_gather.3 = bf16[192,1183]{1,0:T(8,128)(2,1)S(1)} all-gather(bf16[48,1183]{1,0:T(8,128)(2,1)S(1)} %copy.112), channel_id=1, replica_groups=mesh['cell'=8,'band'=4] {'band'}, dimensions={0}, use_global_device_ids=true | all-gather | bytes 567840 | tf_op jit(solution)/shard_map/all_gather | solution.py:127
  210.2 22.7 %psum.7 = f32[48,192]{1,0:T(8,128)S(1)} all-reduce(f32[48,192]{1,0:T(8,128)S(1)} %fusion.97), channel_id=1, replica_groups=mesh['cell'=8,'band'=4] {'cell'}, use_global_device_ids=true, to_apply=%region_10.0 | all-reduce | flops 9216 | bytes 73728 | tf_op jit(solution)/shard_map/psum | solution.py:131
  (141 shorter events, 83.3 us)
Async XLA Ops:
  0.6 30.5 %copy-start = (f32[4,343,343]{2,0,1:T(4,128)S(1)}, f32[4,343,343]{2,0,1:T(4,128)}, u32[]{:S(2)}) copy-start(f32[4,343,343]{2,0,1:T(4,128)} %param.10) | copy-start | bytes 5647156
  9.8 8.8 %copy-start.12 = (f32[32,8]{0,1:T(8,128)S(1)}, f32[32,8]{0,1:T(8,128)}, u32[]{:S(2)}) copy-start(f32[32,8]{0,1:T(8,128)} %param.15) | copy-start | bytes 3076
  9.8 8.8 %copy-start.17 = (s32[32]{0:T(128)S(1)}, s32[32]{0:T(128)}, u32[]{:S(2)}) copy-start(s32[32]{0:T(128)} %param.16) | copy-start | bytes 388
  12.5 11.3 %collective-permute-start.4 = (f32[1,48,16,8]{1,3,2,0:T(8,128)S(1)}, f32[1,48,16,8]{1,3,2,0:T(8,128)S(1)}, u32[]{:S(2)}, u32[]{:S(2)}) collective-permute-start(f32[1,48,16,8]{1,3,2,0:T(8,128)S(1)} %fusion.42), channel_id=1, source_target_pairs={{0,4},{4,8},{8,12},{12,16},{16,20},{20,24},{24,28},{28,0},{1,5},{5... | collective-permute-start | bytes 73736 | tf_op jit(solution)/shard_map/ppermute | solution.py:20
  12.9 10.9 %collective-permute-start.5 = (f32[1,48,16,8]{1,3,2,0:T(8,128)S(1)}, f32[1,48,16,8]{1,3,2,0:T(8,128)S(1)}, u32[]{:S(2)}, u32[]{:S(2)}) collective-permute-start(f32[1,48,16,8]{1,3,2,0:T(8,128)S(1)} %fusion.42), channel_id=1, source_target_pairs={{4,0},{8,4},{12,8},{16,12},{20,16},{24,20},{28,24},{0,28},{5,1},{9... | collective-permute-start | bytes 73736 | tf_op jit(solution)/shard_map/ppermute | solution.py:23
  15.9 14.4 %copy-start.8 = (s32[16]{0:T(128)}, s32[16]{0:T(128)S(1)}, u32[]{:S(2)}) copy-start(s32[16]{0:T(128)S(1)} %get-tuple-element.15) | copy-start | bytes 196
  15.9 70.5 %copy-start.6 = (s32[16]{0:T(128)}, s32[16]{0:T(128)S(1)}, u32[]{:S(2)}) copy-start(s32[16]{0:T(128)S(1)} %get-tuple-element.14) | copy-start | bytes 196
  15.9 3.9 %collective-permute-start = (s32[1,16]{1,0:T(1,128)S(1)}, s32[1,16]{1,0:T(1,128)S(1)}, u32[]{:S(2)}, u32[]{:S(2)}) collective-permute-start(s32[1,16]{1,0:T(1,128)S(1)} %get-tuple-element.16), channel_id=1, source_target_pairs={{0,4},{4,8},{8,12},{12,16},{16,20},{20,24},{24,28},{28,0},{1,5},{5... | collective-permute-start | bytes 200 | tf_op jit(solution)/shard_map/ppermute | solution.py:20
  15.9 3.9 %collective-permute-start.1 = (s32[1,16]{1,0:T(1,128)S(1)}, s32[1,16]{1,0:T(1,128)S(1)}, u32[]{:S(2)}, u32[]{:S(2)}) collective-permute-start(s32[1,16]{1,0:T(1,128)S(1)} %get-tuple-element.16), channel_id=1, source_target_pairs={{4,0},{8,4},{12,8},{16,12},{20,16},{24,20},{28,24},{0,28},{5,1},{9... | collective-permute-start | bytes 200 | tf_op jit(solution)/shard_map/ppermute | solution.py:23
  18.6 11.7 %copy-start.13 = (s32[169,1]{0,1:T(1,128)}, s32[169,1]{0,1:T(1,128)S(1)}, u32[]{:S(2)}) copy-start(s32[169,1]{0,1:T(1,128)S(1)} %get-tuple-element.12) | copy-start | bytes 2032
  18.6 11.7 %copy-start.14 = (s32[169,1]{0,1:T(1,128)}, s32[169,1]{0,1:T(1,128)S(1)}, u32[]{:S(2)}) copy-start(s32[169,1]{0,1:T(1,128)S(1)} %get-tuple-element.13) | copy-start | bytes 2032
  18.6 85.4 %copy-start.5 = (s32[1024]{0:T(1024)}, s32[1024]{0:T(1024)S(1)}, u32[]{:S(2)}) copy-start(s32[1024]{0:T(1024)S(1)} %get-tuple-element.18) | copy-start | bytes 12292
  19.8 3.9 %collective-permute-start.2 = (s32[1,16]{1,0:T(1,128)S(1)}, s32[1,16]{1,0:T(1,128)S(1)}, u32[]{:S(2)}, u32[]{:S(2)}) collective-permute-start(s32[1,16]{1,0:T(1,128)S(1)} %collective-permute-done), channel_id=1, source_target_pairs={{0,4},{4,8},{8,12},{12,16},{16,20},{20,24},{24,28},{28,0},{1,5},{5... | collective-permute-start | bytes 200 | tf_op jit(solution)/shard_map/ppermute | solution.py:20
  19.9 3.9 %collective-permute-start.3 = (s32[1,16]{1,0:T(1,128)S(1)}, s32[1,16]{1,0:T(1,128)S(1)}, u32[]{:S(2)}, u32[]{:S(2)}) collective-permute-start(s32[1,16]{1,0:T(1,128)S(1)} %collective-permute-done.1), channel_id=1, source_target_pairs={{4,0},{8,4},{12,8},{16,12},{20,16},{24,20},{28,24},{0,28},{5,1},{9... | collective-permute-start | bytes 200 | tf_op jit(solution)/shard_map/ppermute | solution.py:23
  23.8 4.8 %collective-permute-start.6 = (f32[1,48,16,8]{1,3,2,0:T(8,128)S(1)}, f32[1,48,16,8]{1,3,2,0:T(8,128)S(1)}, u32[]{:S(2)}, u32[]{:S(2)}) collective-permute-start(f32[1,48,16,8]{1,3,2,0:T(8,128)S(1)} %collective-permute-done.4), channel_id=1, source_target_pairs={{0,4},{4,8},{8,12},{12,16},{16,20},{20,24},{24,28},{28,0},{1,5},{5... | collective-permute-start | bytes 73736 | tf_op jit(solution)/shard_map/ppermute | solution.py:20
  23.9 4.7 %collective-permute-start.7 = (f32[1,48,16,8]{1,3,2,0:T(8,128)S(1)}, f32[1,48,16,8]{1,3,2,0:T(8,128)S(1)}, u32[]{:S(2)}, u32[]{:S(2)}) collective-permute-start(f32[1,48,16,8]{1,3,2,0:T(8,128)S(1)} %collective-permute-done.5), channel_id=1, source_target_pairs={{4,0},{8,4},{12,8},{16,12},{20,16},{24,20},{28,24},{0,28},{5,1},{9... | collective-permute-start | bytes 73736 | tf_op jit(solution)/shard_map/ppermute | solution.py:23
  48.6 5.2 %collective-permute-start.8 = (f32[1,48,169]{1,2,0:T(8,128)}, f32[1,48,169]{1,2,0:T(8,128)}, u32[]{:S(2)}, u32[]{:S(2)}) collective-permute-start(f32[1,48,169]{1,2,0:T(8,128)} %bitcast.185), channel_id=1, source_target_pairs={{0,4},{4,8},{8,12},{12,16},{16,20},{20,24},{24,28},{28,0},{1,5},{5... | collective-permute-start | bytes 97352 | tf_op jit(solution)/shard_map/ppermute | solution.py:20
  51.0 4.8 %collective-permute-start.9 = (f32[1,48,169]{1,2,0:T(8,128)}, f32[1,48,169]{1,2,0:T(8,128)}, u32[]{:S(2)}, u32[]{:S(2)}) collective-permute-start(f32[1,48,169]{1,2,0:T(8,128)} %bitcast.184), channel_id=1, source_target_pairs={{4,0},{8,4},{12,8},{16,12},{20,16},{24,20},{28,24},{0,28},{5,1},{9... | collective-permute-start | bytes 97352 | tf_op jit(solution)/shard_map/ppermute | solution.py:23
  72.1 12.9 %copy-start.9 = (s32[16]{0:T(128)S(1)}, s32[16]{0:T(128)}, u32[]{:S(2)}) copy-start(s32[16]{0:T(128)} %copy-done.8) | copy-start | bytes 196
  74.7 5.2 %collective-permute-start.10 = (f32[1,48,16,8]{1,3,2,0:T(8,128)S(1)}, f32[1,48,16,8]{1,3,2,0:T(8,128)S(1)}, u32[]{:S(2)}, u32[]{:S(2)}) collective-permute-start(f32[1,48,16,8]{1,3,2,0:T(8,128)S(1)} %fusion.45), channel_id=1, source_target_pairs={{0,4},{4,8},{8,12},{12,16},{16,20},{20,24},{24,28},{28,0},{1,5},{5... | collective-permute-start | bytes 73736 | tf_op jit(solution)/shard_map/ppermute | solution.py:20
  75.0 5.0 %collective-permute-start.11 = (f32[1,48,16,8]{1,3,2,0:T(8,128)S(1)}, f32[1,48,16,8]{1,3,2,0:T(8,128)S(1)}, u32[]{:S(2)}, u32[]{:S(2)}) collective-permute-start(f32[1,48,16,8]{1,3,2,0:T(8,128)S(1)} %fusion.45), channel_id=1, source_target_pairs={{4,0},{8,4},{12,8},{16,12},{20,16},{24,20},{28,24},{0,28},{5,1},{9... | collective-permute-start | bytes 73736 | tf_op jit(solution)/shard_map/ppermute | solution.py:23
  79.9 4.6 %collective-permute-start.12 = (f32[1,48,16,8]{1,3,2,0:T(8,128)S(1)}, f32[1,48,16,8]{1,3,2,0:T(8,128)S(1)}, u32[]{:S(2)}, u32[]{:S(2)}) collective-permute-start(f32[1,48,16,8]{1,3,2,0:T(8,128)S(1)} %collective-permute-done.10), channel_id=1, source_target_pairs={{0,4},{4,8},{8,12},{12,16},{16,20},{20,24},{24,28},{28,0},{1,5},{5... | collective-permute-start | bytes 73736 | tf_op jit(solution)/shard_map/ppermute | solution.py:20
  80.0 4.6 %collective-permute-start.13 = (f32[1,48,16,8]{1,3,2,0:T(8,128)S(1)}, f32[1,48,16,8]{1,3,2,0:T(8,128)S(1)}, u32[]{:S(2)}, u32[]{:S(2)}) collective-permute-start(f32[1,48,16,8]{1,3,2,0:T(8,128)S(1)} %collective-permute-done.11), channel_id=1, source_target_pairs={{4,0},{8,4},{12,8},{16,12},{20,16},{24,20},{28,24},{0,28},{5,1},{9... | collective-permute-start | bytes 73736 | tf_op jit(solution)/shard_map/ppermute | solution.py:23
  108.7 5.5 %collective-permute-start.14 = (f32[1,48,169]{1,2,0:T(8,128)}, f32[1,48,169]{1,2,0:T(8,128)}, u32[]{:S(2)}, u32[]{:S(2)}) collective-permute-start(f32[1,48,169]{1,2,0:T(8,128)} %bitcast.183), channel_id=1, source_target_pairs={{0,4},{4,8},{8,12},{12,16},{16,20},{20,24},{24,28},{28,0},{1,5},{5... | collective-permute-start | bytes 97352 | tf_op jit(solution)/shard_map/ppermute | solution.py:20
  108.7 9.1 %collective-permute-start.15 = (f32[1,48,169]{1,2,0:T(8,128)}, f32[1,48,169]{1,2,0:T(8,128)}, u32[]{:S(2)}, u32[]{:S(2)}) collective-permute-start(f32[1,48,169]{1,2,0:T(8,128)} %bitcast.181), channel_id=1, source_target_pairs={{4,0},{8,4},{12,8},{16,12},{20,16},{24,20},{28,24},{0,28},{5,1},{9... | collective-permute-start | bytes 97352 | tf_op jit(solution)/shard_map/ppermute | solution.py:23
  139.9 4.9 %collective-permute-start.16 = (f32[1,48,16,8]{1,3,2,0:T(8,128)}, f32[1,48,16,8]{1,3,2,0:T(8,128)}, u32[]{:S(2)}, u32[]{:S(2)}) collective-permute-start(f32[1,48,16,8]{1,3,2,0:T(8,128)} %fusion.48), channel_id=1, source_target_pairs={{0,4},{4,8},{8,12},{12,16},{16,20},{20,24},{24,28},{28,0},{1,5},{5... | collective-permute-start | bytes 73736 | tf_op jit(solution)/shard_map/ppermute | solution.py:20
  139.9 6.6 %collective-permute-start.17 = (f32[1,48,16,8]{1,3,2,0:T(8,128)}, f32[1,48,16,8]{1,3,2,0:T(8,128)S(1)}, u32[]{:S(2)}, u32[]{:S(2)}) collective-permute-start(f32[1,48,16,8]{1,3,2,0:T(8,128)} %fusion.48), channel_id=1, source_target_pairs={{4,0},{8,4},{12,8},{16,12},{20,16},{24,20},{28,24},{0,28},{5,1},{9... | collective-permute-start | bytes 73736 | tf_op jit(solution)/shard_map/ppermute | solution.py:23
  146.5 4.8 %collective-permute-start.18 = (f32[1,48,16,8]{1,3,2,0:T(8,128)}, f32[1,48,16,8]{1,3,2,0:T(8,128)S(1)}, u32[]{:S(2)}, u32[]{:S(2)}) collective-permute-start(f32[1,48,16,8]{1,3,2,0:T(8,128)} %collective-permute-done.16), channel_id=1, source_target_pairs={{0,4},{4,8},{8,12},{12,16},{16,20},{20,24},{24,28},{28,0},{1,5},{5... | collective-permute-start | bytes 73736 | tf_op jit(solution)/shard_map/ppermute | solution.py:20
  146.5 4.8 %collective-permute-start.19 = (f32[1,48,16,8]{1,3,2,0:T(8,128)S(1)}, f32[1,48,16,8]{1,3,2,0:T(8,128)S(1)}, u32[]{:S(2)}, u32[]{:S(2)}) collective-permute-start(f32[1,48,16,8]{1,3,2,0:T(8,128)S(1)} %collective-permute-done.17), channel_id=1, source_target_pairs={{4,0},{8,4},{12,8},{16,12},{20,16},{24,20},{28,24},{0,28},{5,1},{9... | collective-permute-start | bytes 73736 | tf_op jit(solution)/shard_map/ppermute | solution.py:23
  176.2 5.6 %collective-permute-start.20 = (f32[1,48,169]{1,2,0:T(8,128)}, f32[1,48,169]{1,2,0:T(8,128)S(1)}, u32[]{:S(2)}, u32[]{:S(2)}) collective-permute-start(f32[1,48,169]{1,2,0:T(8,128)} %bitcast.61), channel_id=1, source_target_pairs={{0,4},{4,8},{8,12},{12,16},{16,20},{20,24},{24,28},{28,0},{1,5},{5... | collective-permute-start | bytes 97352 | tf_op jit(solution)/shard_map/ppermute | solution.py:20
  176.2 9.0 %collective-permute-start.21 = (f32[1,48,169]{1,2,0:T(8,128)}, f32[1,48,169]{1,2,0:T(8,128)S(1)}, u32[]{:S(2)}, u32[]{:S(2)}) collective-permute-start(f32[1,48,169]{1,2,0:T(8,128)} %bitcast.182), channel_id=1, source_target_pairs={{4,0},{8,4},{12,8},{16,12},{20,16},{24,20},{28,24},{0,28},{5,1},{9... | collective-permute-start | bytes 97352 | tf_op jit(solution)/shard_map/ppermute | solution.py:23
  191.1 41.8 %copy-start.4 = (f32[48,1183]{0,1:T(8,128)S(1)}, f32[48,1183]{0,1:T(8,128)}, u32[]{:S(2)}) copy-start(f32[48,1183]{0,1:T(8,128)} %get-tuple-element.11) | copy-start | bytes 681412
  (8 other events, 25.6 us)
where the time goes:
time: 236 us; the launch traced here: 235 us
  local copies, waits for them, and re-layouts  64.5 us (27%)
  other arithmetic  54.5 us (23%)
  blocking collectives  39.4 us (17%)
  starting transfers between devices  30 us (13%)
  matrix products  26.4 us (11%)
  waiting for transfers between devices  18.7 us (8%)
    scatter-add x3, other arithmetic, operate(): assembled = jnp.zeros_like(values).at[:, node_map].add(cell_out)  29.2 us
    ppermute x11, starting transfers between devices, extended(): lax.ppermute(lax.slice_in_dim(block, 0, width, axis=dim), axis, backward)  27.8 us
    gather x12, local copies, waits for them, and re-layouts, operate(): cell_vals = values[:, node_map]  26 us
    psum x1, blocking collectives, on_device(): lax.psum(column_block, 'cell')  22.7 us
    ppermute x11, waiting for transfers between devices, extended(): lax.ppermute(lax.slice_in_dim(block, block.shape[dim] - width, None, axis...  18.5 us
    scatter-add x6, other arithmetic, operate(): assembled.at[:, share_pair[0]].add(padded[0]).at[:, share_pair[1]]  18.2 us
    all_gather x1, blocking collectives, on_device(): lax.all_gather(zed, 'band', axis=0, tiled=True)  16.7 us
    add x6, local copies, waits for them, and re-layouts, operate(): cell_out + jnp.einsum('bei,ec->bci', added_terms, onehot_cell, precision=...  12.3 us
  transfers between devices with their start and end apart: 22, of which 12 were waited for; matrix products, arithmetic and copies ran while one was open for 6% of the time, Pallas kernels for 0%

commit v1 on v0

v1 whole, which is shorter than its diff:
```python
import functools
import math

import jax
import jax.numpy as jnp
from jax import lax
from jax.experimental import pallas as pl
from jax.experimental.pallas import tpu as pltpu
from jax.sharding import PartitionSpec as P

CENTER = 1.0
HALF_WIDTH = 1.0
LOWEST = -0.5
MESH = pl.DeviceIdType.MESH
F32 = jnp.float32
BF16 = jnp.bfloat16
NN = (((1,), (0,)), ((), ()))
NT = (((1,), (1,)), ((), ()))


def filter_terms():
    sigma_now = HALF_WIDTH / (LOWEST - CENTER)
    gamma_ratio = 2.0 / sigma_now
    terms = [(sigma_now / HALF_WIDTH, 0.0)]
    for turn_index in range(2):
        sigma_next = 1.0 / (gamma_ratio - sigma_now)
        terms.append((2.0 * sigma_next / HALF_WIDTH, sigma_now * sigma_next))
        sigma_now = sigma_next
    return terms


def up(size, unit):
    return -(-size // unit) * unit


def mm(left, right, dims):
    return lax.dot_general(left, right, dims, preferred_element_type=F32)


def halves(value):
    high = value.astype(BF16)
    low = (value - high.astype(F32)).astype(BF16)
    return high, low


def split_rows(value):
    return jnp.concatenate(halves(value), axis=0)


def join_rows(value):
    rows = value.shape[0] // 2
    return value[:rows] + value[rows:]


def iota(shape, axis):
    return lax.broadcasted_iota(jnp.int32, shape, axis)


def as_column(row):
    size = row.shape[1]
    eye = iota((size, size), 0) == iota((size, size), 1)
    return jnp.sum(jnp.where(eye, row, 0.0), axis=1, keepdims=True)


def as_row(column):
    size = column.shape[0]
    eye = iota((size, size), 0) == iota((size, size), 1)
    return jnp.sum(jnp.where(eye, column, 0.0), axis=0, keepdims=True)


def one_hot(mask):
    return jnp.where(mask, 1.0, 0.0).astype(BF16)


OFFSETS = (1, -1, 2, -2)


def kernel(
    n_cell,
    n_band,
    waves,
    cell_matrix,
    node_map,
    share_list,
    contacts,
    proj_values,
    coupling,
    proj_count,
    mass,
    filtered,
    gram,
    spots,
    pairs,
    lanes_of,
    faces_of,
    face_spot,
    projs,
    proj_node,
    mixed,
    vals,
    sums,
    y0,
    y1,
    y2,
    ids,
    near_ids,
    coeff_own,
    coeff_near,
    face_send,
    face_recv,
    zeds,
    grams,
    id_sems,
    coeff_sems,
    face_sems,
    zed_sems,
    gram_sems,
):
    me = lax.axis_index("cell")
    group = lax.axis_index("band")
    bands, nodes = waves.shape
    cells, cell_nodes = node_map.shape
    face = share_list.shape[1]
    entries, slots, _ = proj_values.shape
    terms = entries * slots
    atoms = coupling.shape[0]
    node_pad = y0.shape[1]
    cell_pad = lanes_of.shape[1]
    face_pad = faces_of.shape[1]

    def peer(offset):
        return {"cell": lax.rem(me + (offset + n_cell), n_cell)}

    def band_peer(offset):
        return {"band": lax.rem(group + offset, n_band)}

    barrier = pltpu.get_barrier_semaphore()
    for offset in range(1, n_cell):
        pl.semaphore_signal(barrier, inc=1, device_id=peer(offset), device_id_type=MESH)
    for offset in range(1, n_band):
        pl.semaphore_signal(barrier, inc=1, device_id=band_peer(offset), device_id_type=MESH)

    pick = iota((terms, entries), 0) // slots == iota((terms, entries), 1)
    held = contacts[...].astype(F32)
    cell_col = jnp.sum(jnp.where(pick, held[0:1], 0.0), axis=1, keepdims=True)
    atom_col = jnp.sum(jnp.where(pick, held[1:2], 0.0), axis=1, keepdims=True)
    slot_col = (iota((terms, 1), 0) % slots).astype(F32)
    id_col = atom_col * slots + slot_col
    ids[...] = jnp.broadcast_to(as_row(id_col), ids.shape)

    pl.semaphore_wait(barrier, n_cell - 1 + n_band - 1)
    started = []
    for k, offset in enumerate(OFFSETS):
        copy = pltpu.make_async_remote_copy(
            ids, near_ids.at[k], id_sems.at[0, k], id_sems.at[1, k],
            device_id=peer(offset), device_id_type=MESH,
        )
        copy.start()
        started.append(copy)

    count_col = as_column(proj_count[...].astype(F32))
    kept = iota((atoms, slots), 1).astype(F32) < count_col
    scales = jnp.where(kept, coupling[...], 0.0)
    atom_hot = jnp.where(atom_col == iota((terms, atoms), 1).astype(F32), 1.0, 0.0)
    scale_all = lax.dot_general(
        atom_hot, scales, NN, precision=lax.Precision.HIGHEST, preferred_element_type=F32
    )
    own_slot = iota((terms, slots), 1).astype(F32) == slot_col
    scale_row = as_row(jnp.sum(jnp.where(own_slot, scale_all, 0.0), axis=1, keepdims=True))

    lanes_of[...] = jnp.full(lanes_of.shape, -1, jnp.int32)
    lanes_of[:, :cell_nodes] = node_map[...]
    faces_of[...] = jnp.full(faces_of.shape, -2, jnp.int32)
    faces_of[:, :face] = share_list[...]
    for c in range(cells):
        spots[:, c * cell_pad : (c + 1) * cell_pad] = one_hot(
            iota((node_pad, cell_pad), 0) == lanes_of[c : c + 1, :]
        )
    for side in range(2):
        face_row = faces_of[side : side + 1, :]
        face_col = as_column(face_row.astype(F32)).astype(jnp.int32)
        here = slice(side * face_pad, (side + 1) * face_pad)
        face_spot[:, here] = one_hot(iota((node_pad, face_pad), 0) == face_row)
        for c in range(cells):
            pairs[here, c * cell_pad : (c + 1) * cell_pad] = one_hot(
                face_col == lanes_of[c : c + 1, :]
            )

    projs[...] = jnp.zeros(projs.shape, BF16)
    flat_high, flat_low = halves(proj_values[...].reshape(terms, cell_nodes))
    for c in range(cells):
        lanes = slice(c * cell_pad, c * cell_pad + cell_nodes)
        inside = cell_col == float(c)
        projs[0:terms, lanes] = jnp.where(inside, flat_high.astype(F32), 0.0).astype(BF16)
        projs[terms : 2 * terms, lanes] = jnp.where(inside, flat_low.astype(F32), 0.0).astype(BF16)
    proj_node[...] = mm(projs[...], spots[...], NT).astype(BF16)

    mixed[...] = jnp.zeros(mixed.shape, BF16)
    for c in range(cells):
        high, low = halves(cell_matrix[c])
        mixed[c, 0:cell_nodes, 0:cell_nodes] = high
        mixed[c, cell_pad : cell_pad + cell_nodes, 0:cell_nodes] = low

    y0[...] = jnp.zeros(y0.shape, F32)
    y0[:, :nodes] = waves[...]

    for copy in started:
        copy.wait()
    sums[:, 0:terms] = one_hot(id_col == ids[0:1, :])
    for k in range(len(OFFSETS)):
        sums[:, (k + 1) * terms : (k + 2) * terms] = one_hot(id_col == near_ids[k, 0:1, :])

    previous, current = None, y0[...]
    for turn, (lead, back) in enumerate(filter_terms()):
        values = split_rows(current)
        product = mm(values, proj_node[...], NT)
        product = join_rows(product)
        coeff_own[turn] = product[:, :terms] + product[:, terms:]
        coeff_copies = []
        for k, offset in enumerate(OFFSETS):
            copy = pltpu.make_async_remote_copy(
                coeff_own.at[turn], coeff_near.at[turn, k],
                coeff_sems.at[0, turn, k], coeff_sems.at[1, turn, k],
                device_id=peer(offset), device_id_type=MESH,
            )
            copy.start()
            coeff_copies.append(copy)

        gathered = mm(values, spots[...], NN).astype(BF16)
        for c in range(cells):
            lanes = slice(c * cell_pad, (c + 1) * cell_pad)
            product = join_rows(mm(gathered[:, lanes], mixed[c], NT))
            vals[:, lanes] = product[:, :cell_pad] + product[:, cell_pad:]

        for copy in coeff_copies:
            copy.wait()
        near = jnp.concatenate(
            [coeff_own[turn]] + [coeff_near[turn, k] for k in range(len(OFFSETS))], axis=1
        )
        scaled = split_rows(join_rows(mm(split_rows(near), sums[...], NT)) * scale_row)
        added = mm(jnp.concatenate([scaled, scaled], axis=1), projs[...], NN)
        cell_out = split_rows(vals[...] + join_rows(added))

        face_vals = join_rows(mm(cell_out, pairs[...], NT))
        face_copies = []
        for side in range(2):
            face_send[turn, side] = face_vals[:, side * face_pad : (side + 1) * face_pad]
            copy = pltpu.make_async_remote_copy(
                face_send.at[turn, side], face_recv.at[turn, 1 - side],
                face_sems.at[0, turn, side], face_sems.at[1, turn, side],
                device_id=peer(2 * side - 1), device_id_type=MESH,
            )
            copy.start()
            face_copies.append(copy)
        assembled = join_rows(mm(cell_out, spots[...], NT))
        assembled = lead * (assembled - CENTER * current)
        if previous is not None:
            assembled = assembled - back * previous
        for copy in face_copies:
            copy.wait()
        arrived = jnp.concatenate([face_recv[turn, 0], face_recv[turn, 1]], axis=1)
        arrived = join_rows(mm(split_rows(arrived), face_spot[...], NT))
        held_ref = (y1, y2, y1)[turn]
        previous = current
        held_ref[...] = assembled + lead * arrived
        current = held_ref[...]

    filtered[...] = current[:, :nodes]
    shared = mm(jnp.ones((16, face_pad), BF16), face_spot[:, 0:face_pad], NT)[0:1]
    y0[...] = jnp.zeros(y0.shape, F32)
    y0[0:1, :nodes] = jnp.sqrt(mass[...])
    weight = (1.0 - shared) * y0[0:1, :]
    zeds[group] = (current * weight).astype(BF16)
    copies = []
    for offset in range(1, n_band):
        copy = pltpu.make_async_remote_copy(
            zeds.at[group], zeds.at[group], zed_sems.at[0, offset - 1], zed_sems.at[1, offset - 1],
            device_id=band_peer(offset), device_id_type=MESH,
        )
        copy.start()
        copies.append(copy)
    for copy in copies:
        copy.wait_recv()
    grams[me] = mm(zeds[group], zeds[...].reshape(n_band * bands, node_pad), NT)
    for offset in range(1, n_cell):
        copy = pltpu.make_async_remote_copy(
            grams.at[me], grams.at[me], gram_sems.at[0, offset - 1], gram_sems.at[1, offset - 1],
            device_id=peer(offset), device_id_type=MESH,
        )
        copy.start()
        copies.append(copy)
    for copy in copies[n_band - 1 :]:
        copy.wait_recv()
    total = grams[0]
    for part in range(1, n_cell):
        total = total + grams[part]
    total = total / math.sqrt(n_cell * nodes)
    rows = group * bands + iota(total.shape, 0)
    gram[...] = jnp.where(rows == iota(total.shape, 1), 0.0, total)
    for copy in copies:
        copy.wait_send()


def on_device(
    waves, cell_matrix, node_map, share_list, contacts, proj_values, coupling, proj_count, mass
):
    n_cell = lax.axis_size("cell")
    n_band = lax.axis_size("band")
    bands, nodes = waves.shape
    cells, cell_nodes = node_map.shape
    entries, slots, _ = proj_values.shape
    terms = entries * slots
    node_pad = up(nodes, 128)
    cell_pad = up(cell_nodes, 128)
    face_pad = up(share_list.shape[2], 128)
    wide = cells * cell_pad
    peers = len(OFFSETS)
    dma = pltpu.SemaphoreType.DMA
    return pl.pallas_call(
        functools.partial(kernel, n_cell, n_band),
        out_shape=(
            jax.ShapeDtypeStruct((bands, nodes), F32),
            jax.ShapeDtypeStruct((bands, n_band * bands), F32),
        ),
        in_specs=[pl.BlockSpec(memory_space=pltpu.VMEM)] * 9,
        out_specs=(pl.BlockSpec(memory_space=pltpu.VMEM),) * 2,
        scratch_shapes=[
            pltpu.VMEM((node_pad, wide), BF16),
            pltpu.VMEM((2 * face_pad, wide), BF16),
            pltpu.VMEM((cells, cell_pad), jnp.int32),
            pltpu.VMEM((2, face_pad), jnp.int32),
            pltpu.VMEM((node_pad, 2 * face_pad), BF16),
            pltpu.VMEM((2 * terms, wide), BF16),
            pltpu.VMEM((2 * terms, node_pad), BF16),
            pltpu.VMEM((cells, 2 * cell_pad, cell_pad), BF16),
            pltpu.VMEM((bands, wide), F32),
            pltpu.VMEM((terms, (1 + peers) * terms), BF16),
            pltpu.VMEM((bands, node_pad), F32),
            pltpu.VMEM((bands, node_pad), F32),
            pltpu.VMEM((bands, node_pad), F32),
            pltpu.VMEM((8, terms), F32),
            pltpu.VMEM((peers, 8, terms), F32),
            pltpu.VMEM((3, bands, terms), F32),
            pltpu.VMEM((3, peers, bands, terms), F32),
            pltpu.VMEM((3, 2, bands, face_pad), F32),
            pltpu.VMEM((3, 2, bands, face_pad), F32),
            pltpu.VMEM((n_band, bands, node_pad), BF16),
            pltpu.VMEM((n_cell, bands, n_band * bands), F32),
            dma((2, peers)),
            dma((2, 3, peers)),
            dma((2, 3, 2)),
            dma((2, n_band - 1)),
            dma((2, n_cell - 1)),
        ],
        compiler_params=pltpu.CompilerParams(
            collective_id=0, has_side_effects=True, vmem_limit_bytes=48 * 1024 * 1024
        ),
    )(
        waves,
        cell_matrix,
        node_map,
        share_list.reshape(share_list.shape[1:]),
        contacts,
        proj_values,
        coupling,
        proj_count.reshape(1, -1),
        mass.reshape(1, -1),
    )


def solution(mesh):
    return jax.shard_map(
        on_device,
        mesh=mesh,
        in_specs=(
            P("band", "cell"),
            P("cell", None, None),
            P("cell", None),
            P("cell", None, None),
            P(None, "cell"),
            P("cell", None, None),
            P(),
            P(),
            P("cell"),
        ),
        out_specs=(P("band", "cell"), P("band", None)),
        check_vma=False,
    )
```

time: 236 us -> 56.9 us (0.24)
  local copies, waits for them, and re-layouts: 64.5 us -> 4.61 us
  other arithmetic: 54.5 us -> 0 us
  Pallas kernels: 0 us -> 50.6 us
  blocking collectives: 39.4 us -> 0 us
  starting transfers between devices: 30 us -> 0 us
  matrix products: 26.4 us -> 0 us
  waiting for transfers between devices: 18.7 us -> 0 us
    pallas_call x0 -> x1, Pallas kernels: none -> 50.6 us  [on_device(): pl.pallas_call(functools.partial(kernel, n_cell, n_band), out_shape=(jax....]
    scatter-add x9 -> x0, other arithmetic: 47.4 us -> none  [the longest x3 29.2 us: operate(): assembled = jnp.zeros_like(values).at[:, node_map].add(cell_out)]
    gather x21 -> x0, local copies, waits for them, and re-layouts: 45.2 us -> none  [the longest x12 26 us: operate(): cell_vals = values[:, node_map]]
    ppermute x22 -> x0, starting transfers between devices: 30 us -> none  [the longest x11 27.8 us: extended(): lax.ppermute(lax.slice_in_dim(block, 0, width, axis=dim), axis, backward)]
    dot_general x19 -> x0, matrix products: 26.4 us -> none  [the longest x3 8.58 us: operate(): jnp.einsum('bei,epi->bep', entry_vals, proj_values, precision=PRECISE)]
    psum x1 -> x0, blocking collectives: 22.7 us -> none  [on_device(): lax.psum(column_block, 'cell')]
    ppermute x22 -> x0, waiting for transfers between devices: 18.7 us -> none  [the longest x11 18.5 us: extended(): lax.ppermute(lax.slice_in_dim(block, block.shape[dim] - width, None, axis...]
    all_gather x1 -> x0, blocking collectives: 16.7 us -> none  [on_device(): lax.all_gather(zed, 'band', axis=0, tiled=True)]
  transfers between devices with their start and end apart: 22 -> 0, of which waited for: 12 -> 0; matrix products, arithmetic and copies ran while one was open for 6% -> 0% of each run, Pallas kernels for 0% -> 0%
where the time goes in v1:
time: 56.9 us; the launch traced here: 56 us
  Pallas kernels  50.6 us (89%)
  local copies, waits for them, and re-layouts  4.61 us (8%)
  between operations  0.72 us (1%)
    pallas_call x1, Pallas kernels, on_device(): pl.pallas_call(functools.partial(kernel, n_cell, n_band), out_shape=(jax....  50.6 us
    unnamed x16, local copies, waits for them, and re-layouts  3.91 us

profile of v1, /device:TPU:0, one launch (start us, length us, event | category | flops | bytes accessed | tf_op | source)
XLA Modules:
  0.0 56.0 jit_solution(6206973410535454558)
XLA Ops:
  0.6 0.7 %reshape.15.mass = f32[1,1183]{1,0:T(1,128)S(1)} reshape(f32[1183]{0:T(1024)} %param.17) | data formatting | bytes 9464 | tf_op jit(solution)/shard_map/reshape | solution.py:367
  1.3 0.8 %copy.12.coupling = f32[32,8]{1,0:T(8,128)S(1)} copy(f32[32,8]{0,1:T(8,128)} %param.15) | data formatting | bytes 2048 | tf_op args[6]
  2.1 0.0 copy-start
  2.1 0.0 copy-start.1
  2.1 0.0 copy-start.2
  2.1 0.0 copy-start.3
  2.1 0.0 copy-start.4
  2.1 0.0 copy-start.5
  2.1 1.8 %copy.11.cell_matrix = f32[4,343,343]{2,1,0:T(8,128)S(1)} copy(f32[4,343,343]{2,0,1:T(4,128)} %param.10) | data formatting | bytes 3764768 | tf_op args[1]
  3.9 0.0 copy-done
  4.0 0.0 copy-done.1
  4.0 0.0 copy-done.2
  4.0 0.0 copy-done.3
  4.0 0.0 copy-done.4
  4.0 0.0 copy-done.5
  4.0 50.6 %shard_map.104 = (f32[48,1183]{1,0:T(8,128)S(1)}, f32[48,192]{1,0:T(8,128)S(1)}) custom-call(f32[48,1183]{1,0:T(8,128)S(1)} %copy-done, f32[4,343,343]{2,1,0:T(8,128)S(1)} %copy.11.cell_matrix, s32[4,343]{1,0:T(4,128)S(1)} %copy-done.2, s32[2,169]{1,0:T(2,128)S(1)} %bitcast.2, s32[2,16]{1,0:T(2,128)S(1)} %copy-done.4, f32[16,8,343]{2,1,0:T(8,128)S(1)} %copy-done.1, ...), custom_call_target="tpu_custom_call" | custom-call | tf_op jit(solution)/shard_map/pallas_call | solution.py:319
  54.7 0.7 %copy.15 = f32[48,1183]{1,0:T(8,128)} copy(f32[48,1183]{1,0:T(8,128)S(1)} %get-tuple-element.4) | data formatting | bytes 454272
  55.4 0.6 %copy.16 = f32[48,192]{1,0:T(8,128)} copy(f32[48,192]{1,0:T(8,128)S(1)} %get-tuple-element.5) | data formatting | bytes 73728
Async XLA Ops:
  2.1 1.9 %copy-start = (f32[48,1183]{1,0:T(8,128)S(1)}, f32[48,1183]{1,0:T(8,128)}, u32[]{:S(2)}) copy-start(f32[48,1183]{1,0:T(8,128)} %waves.1) | copy-start | bytes 681412
  2.1 1.9 %copy-start.1 = (f32[16,8,343]{2,1,0:T(8,128)S(1)}, f32[16,8,343]{2,1,0:T(8,128)}, u32[]{:S(2)}) copy-start(f32[16,8,343]{2,1,0:T(8,128)} %proj_values.1) | copy-start | bytes 526852
  2.1 1.9 %copy-start.2 = (s32[4,343]{1,0:T(4,128)S(1)}, s32[4,343]{1,0:T(4,128)}, u32[]{:S(2)}) copy-start(s32[4,343]{1,0:T(4,128)} %node_map.1) | copy-start | bytes 16468
  2.1 1.9 %copy-start.3 = (s32[1,2,169]{2,1,0:T(2,128)S(1)}, s32[1,2,169]{2,1,0:T(2,128)}, u32[]{:S(2)}) copy-start(s32[1,2,169]{2,1,0:T(2,128)} %param.12) | copy-start | bytes 4060
  2.1 1.9 %copy-start.4 = (s32[2,16]{1,0:T(2,128)S(1)}, s32[2,16]{1,0:T(2,128)}, u32[]{:S(2)}) copy-start(s32[2,16]{1,0:T(2,128)} %contacts.1) | copy-start | bytes 388
  2.1 1.9 %copy-start.5 = (s32[32]{0:T(128)S(1)}, s32[32]{0:T(128)}, u32[]{:S(2)}) copy-start(s32[32]{0:T(128)} %param.16) | copy-start | bytes 388

commit v2 on v1

--- a/solution.py
+++ b/solution.py
@@ -108,12 +108,16 @@
     coeff_near,
     face_send,
     face_recv,
+    zed_half,
     zeds,
+    block_send,
+    block_recv,
     grams,
     id_sems,
     coeff_sems,
     face_sems,
     zed_sems,
+    block_sems,
     gram_sems,
 ):
     me = lax.axis_index("cell")
@@ -270,18 +274,47 @@
     y0[...] = jnp.zeros(y0.shape, F32)
     y0[0:1, :nodes] = jnp.sqrt(mass[...])
     weight = (1.0 - shared) * y0[0:1, :]
-    zeds[group] = (current * weight).astype(BF16)
+    zed = (current * weight).astype(BF16)
+    half = zed_half.shape[2]
+    zed_half[0] = zed[:, :half]
+    zed_half[1] = zed[:, half:]
+    zeds[group] = zed[:, :half]
     copies = []
     for offset in range(1, n_band):
         copy = pltpu.make_async_remote_copy(
-            zeds.at[group], zeds.at[group], zed_sems.at[0, offset - 1], zed_sems.at[1, offset - 1],
+            zed_half.at[(group + offset) // n_band], zeds.at[group],
+            zed_sems.at[0, offset - 1], zed_sems.at[1, offset - 1],
             device_id=band_peer(offset), device_id_type=MESH,
         )
         copy.start()
         copies.append(copy)
+    own_block = mm(zed, zed, NT)
     for copy in copies:
         copy.wait_recv()
-    grams[me] = mm(zeds[group], zeds[...].reshape(n_band * bands, node_pad), NT)
+    others = zeds[...].reshape(n_band * bands, half)
+    turned_first = mm(others, zed_half[0], NT)
+    turned_second = mm(others, zed_half[1], NT)
+    below = iota(turned_first.shape, 0) < group * bands
+    block_send[...] = jnp.where(below, turned_first, turned_second).reshape(block_send.shape)
+    block_copies = []
+    for offset in range(1, n_band):
+        copy = pltpu.make_async_remote_copy(
+            block_send.at[lax.rem(group + offset, n_band)], block_recv.at[group],
+            block_sems.at[0, offset - 1], block_sems.at[1, offset - 1],
+            device_id=band_peer(offset), device_id_type=MESH,
+        )
+        copy.start()
+        block_copies.append(copy)
+    block_recv[group] = own_block
+    straight_first = mm(zed_half[0], others, NT)
+    straight_second = mm(zed_half[1], others, NT)
+    places = iota(straight_first.shape, 1)
+    straight = jnp.where(places < group * bands, straight_first, straight_second)
+    inside = jnp.logical_and(places >= group * bands, places < (group + 1) * bands)
+    straight = jnp.where(inside, 0.0, straight)
+    for copy in block_copies:
+        copy.wait()
+    grams[me] = straight + jnp.concatenate([block_recv[j] for j in range(n_band)], axis=1)
     for offset in range(1, n_cell):
         copy = pltpu.make_async_remote_copy(
             grams.at[me], grams.at[me], gram_sems.at[0, offset - 1], gram_sems.at[1, offset - 1],
@@ -310,7 +343,7 @@
     cells, cell_nodes = node_map.shape
     entries, slots, _ = proj_values.shape
     terms = entries * slots
-    node_pad = up(nodes, 128)
+    node_pad = up(nodes, 256)
     cell_pad = up(cell_nodes, 128)
     face_pad = up(share_list.shape[2], 128)
     wide = cells * cell_pad
@@ -344,11 +377,15 @@
             pltpu.VMEM((3, peers, bands, terms), F32),
             pltpu.VMEM((3, 2, bands, face_pad), F32),
             pltpu.VMEM((3, 2, bands, face_pad), F32),
-            pltpu.VMEM((n_band, bands, node_pad), BF16),
+            pltpu.VMEM((2, bands, node_pad // 2), BF16),
+            pltpu.VMEM((n_band, bands, node_pad // 2), BF16),
+            pltpu.VMEM((n_band, bands, bands), F32),
+            pltpu.VMEM((n_band, bands, bands), F32),
             pltpu.VMEM((n_cell, bands, n_band * bands), F32),
             dma((2, peers)),
             dma((2, 3, peers)),
             dma((2, 3, 2)),
+            dma((2, n_band - 1)),
             dma((2, n_band - 1)),
             dma((2, n_cell - 1)),
         ],

time: 56.9 us -> 57 us (level); the launches traced: 56 us -> 56.7 us
  Pallas kernels: 50.6 us -> 51.4 us
    pallas_call x1, Pallas kernels: 50.6 us -> 51.4 us  [on_device(): pl.pallas_call(functools.partial(kernel, n_cell, n_band), out_shape=(jax....]
where the time goes in v2:
time: 57 us; the launch traced here: 56.7 us
  Pallas kernels  51.4 us (90%)
  local copies, waits for them, and re-layouts  4.61 us (8%)
  between operations  0.72 us (1%)
    pallas_call x1, Pallas kernels, on_device(): pl.pallas_call(functools.partial(kernel, n_cell, n_band), out_shape=(jax....  51.4 us
    unnamed x16, local copies, waits for them, and re-layouts  3.91 us

profile of v2, /device:TPU:0, one launch (start us, length us, event | category | flops | bytes accessed | tf_op | source)
XLA Modules:
  0.0 56.7 jit_solution(12041759073918214516)
XLA Ops:
  0.6 0.7 %reshape.15.mass = f32[1,1183]{1,0:T(1,128)S(1)} reshape(f32[1183]{0:T(1024)} %param.17) | data formatting | bytes 9464 | tf_op jit(solution)/shard_map/reshape | solution.py:404
  1.3 0.8 %copy.12.coupling = f32[32,8]{1,0:T(8,128)S(1)} copy(f32[32,8]{0,1:T(8,128)} %param.15) | data formatting | bytes 2048 | tf_op args[6]
  2.1 0.0 copy-start
  2.1 0.0 copy-start.1
  2.1 0.0 copy-start.2
  2.1 0.0 copy-start.3
  2.1 0.0 copy-start.4
  2.1 0.0 copy-start.5
  2.1 1.8 %copy.11.cell_matrix = f32[4,343,343]{2,1,0:T(8,128)S(1)} copy(f32[4,343,343]{2,0,1:T(4,128)} %param.10) | data formatting | bytes 3764768 | tf_op args[1]
  3.9 0.0 copy-done
  4.0 0.0 copy-done.1
  4.0 0.0 copy-done.2
  4.0 0.0 copy-done.3
  4.0 0.0 copy-done.4
  4.0 0.0 copy-done.5
  4.0 51.4 %shard_map.104 = (f32[48,1183]{1,0:T(8,128)S(1)}, f32[48,192]{1,0:T(8,128)S(1)}) custom-call(f32[48,1183]{1,0:T(8,128)S(1)} %copy-done, f32[4,343,343]{2,1,0:T(8,128)S(1)} %copy.11.cell_matrix, s32[4,343]{1,0:T(4,128)S(1)} %copy-done.2, s32[2,169]{1,0:T(2,128)S(1)} %bitcast.2, s32[2,16]{1,0:T(2,128)S(1)} %copy-done.4, f32[16,8,343]{2,1,0:T(8,128)S(1)} %copy-done.1, ...), custom_call_target="tpu_custom_call" | custom-call | tf_op jit(solution)/shard_map/pallas_call | solution.py:352
  55.4 0.7 %copy.15 = f32[48,1183]{1,0:T(8,128)} copy(f32[48,1183]{1,0:T(8,128)S(1)} %get-tuple-element.4) | data formatting | bytes 454272
  56.1 0.6 %copy.16 = f32[48,192]{1,0:T(8,128)} copy(f32[48,192]{1,0:T(8,128)S(1)} %get-tuple-element.5) | data formatting | bytes 73728
Async XLA Ops:
  2.1 1.9 %copy-start = (f32[48,1183]{1,0:T(8,128)S(1)}, f32[48,1183]{1,0:T(8,128)}, u32[]{:S(2)}) copy-start(f32[48,1183]{1,0:T(8,128)} %waves.1) | copy-start | bytes 681412
  2.1 1.9 %copy-start.1 = (f32[16,8,343]{2,1,0:T(8,128)S(1)}, f32[16,8,343]{2,1,0:T(8,128)}, u32[]{:S(2)}) copy-start(f32[16,8,343]{2,1,0:T(8,128)} %proj_values.1) | copy-start | bytes 526852
  2.1 1.9 %copy-start.2 = (s32[4,343]{1,0:T(4,128)S(1)}, s32[4,343]{1,0:T(4,128)}, u32[]{:S(2)}) copy-start(s32[4,343]{1,0:T(4,128)} %node_map.1) | copy-start | bytes 16468
  2.1 1.9 %copy-start.3 = (s32[1,2,169]{2,1,0:T(2,128)S(1)}, s32[1,2,169]{2,1,0:T(2,128)}, u32[]{:S(2)}) copy-start(s32[1,2,169]{2,1,0:T(2,128)} %param.12) | copy-start | bytes 4060
  2.1 1.9 %copy-start.4 = (s32[2,16]{1,0:T(2,128)S(1)}, s32[2,16]{1,0:T(2,128)}, u32[]{:S(2)}) copy-start(s32[2,16]{1,0:T(2,128)} %contacts.1) | copy-start | bytes 388
  2.1 1.9 %copy-start.5 = (s32[32]{0:T(128)S(1)}, s32[32]{0:T(128)}, u32[]{:S(2)}) copy-start(s32[32]{0:T(128)} %param.16) | copy-start | bytes 388

commit v3 on v2

--- a/solution.py
+++ b/solution.py
@@ -102,6 +102,7 @@
     y0,
     y1,
     y2,
+    roots,
     ids,
     near_ids,
     coeff_own,
@@ -127,7 +128,7 @@
     face = share_list.shape[1]
     entries, slots, _ = proj_values.shape
     terms = entries * slots
-    atoms = coupling.shape[0]
+    atoms = coupling.shape[1]
     node_pad = y0.shape[1]
     cell_pad = lanes_of.shape[1]
     face_pad = faces_of.shape[1]
@@ -162,16 +163,6 @@
         copy.start()
         started.append(copy)
 
-    count_col = as_column(proj_count[...].astype(F32))
-    kept = iota((atoms, slots), 1).astype(F32) < count_col
-    scales = jnp.where(kept, coupling[...], 0.0)
-    atom_hot = jnp.where(atom_col == iota((terms, atoms), 1).astype(F32), 1.0, 0.0)
-    scale_all = lax.dot_general(
-        atom_hot, scales, NN, precision=lax.Precision.HIGHEST, preferred_element_type=F32
-    )
-    own_slot = iota((terms, slots), 1).astype(F32) == slot_col
-    scale_row = as_row(jnp.sum(jnp.where(own_slot, scale_all, 0.0), axis=1, keepdims=True))
-
     lanes_of[...] = jnp.full(lanes_of.shape, -1, jnp.int32)
     lanes_of[:, :cell_nodes] = node_map[...]
     faces_of[...] = jnp.full(faces_of.shape, -2, jnp.int32)
@@ -180,16 +171,6 @@
         spots[:, c * cell_pad : (c + 1) * cell_pad] = one_hot(
             iota((node_pad, cell_pad), 0) == lanes_of[c : c + 1, :]
         )
-    for side in range(2):
-        face_row = faces_of[side : side + 1, :]
-        face_col = as_column(face_row.astype(F32)).astype(jnp.int32)
-        here = slice(side * face_pad, (side + 1) * face_pad)
-        face_spot[:, here] = one_hot(iota((node_pad, face_pad), 0) == face_row)
-        for c in range(cells):
-            pairs[here, c * cell_pad : (c + 1) * cell_pad] = one_hot(
-                face_col == lanes_of[c : c + 1, :]
-            )
-
     projs[...] = jnp.zeros(projs.shape, BF16)
     flat_high, flat_low = halves(proj_values[...].reshape(terms, cell_nodes))
     for c in range(cells):
@@ -199,20 +180,8 @@
         projs[terms : 2 * terms, lanes] = jnp.where(inside, flat_low.astype(F32), 0.0).astype(BF16)
     proj_node[...] = mm(projs[...], spots[...], NT).astype(BF16)
 
-    mixed[...] = jnp.zeros(mixed.shape, BF16)
-    for c in range(cells):
-        high, low = halves(cell_matrix[c])
-        mixed[c, 0:cell_nodes, 0:cell_nodes] = high
-        mixed[c, cell_pad : cell_pad + cell_nodes, 0:cell_nodes] = low
-
     y0[...] = jnp.zeros(y0.shape, F32)
     y0[:, :nodes] = waves[...]
-
-    for copy in started:
-        copy.wait()
-    sums[:, 0:terms] = one_hot(id_col == ids[0:1, :])
-    for k in range(len(OFFSETS)):
-        sums[:, (k + 1) * terms : (k + 2) * terms] = one_hot(id_col == near_ids[k, 0:1, :])
 
     previous, current = None, y0[...]
     for turn, (lead, back) in enumerate(filter_terms()):
@@ -229,6 +198,44 @@
             )
             copy.start()
             coeff_copies.append(copy)
+
+        if turn == 0:
+            mixed[...] = jnp.zeros(mixed.shape, BF16)
+            for c in range(cells):
+                high, low = halves(cell_matrix[c])
+                mixed[c, 0:cell_nodes, 0:cell_nodes] = high
+                mixed[c, cell_pad : cell_pad + cell_nodes, 0:cell_nodes] = low
+
+            for side in range(2):
+                face_row = faces_of[side : side + 1, :]
+                face_col = as_column(face_row.astype(F32)).astype(jnp.int32)
+                here = slice(side * face_pad, (side + 1) * face_pad)
+                face_spot[:, here] = one_hot(iota((node_pad, face_pad), 0) == face_row)
+                for c in range(cells):
+                    pairs[here, c * cell_pad : (c + 1) * cell_pad] = one_hot(
+                        face_col == lanes_of[c : c + 1, :]
+                    )
+
+            for copy in started:
+                copy.wait()
+            sums[:, 0:terms] = one_hot(id_col == ids[0:1, :])
+            for k in range(len(OFFSETS)):
+                sums[:, (k + 1) * terms : (k + 2) * terms] = one_hot(id_col == near_ids[k, 0:1, :])
+
+            levels = iota((slots, atoms), 0)
+            scales = jnp.where(levels < proj_count[...], coupling[...], 0.0)
+            atom_hot = jnp.where(atom_col == iota((terms, atoms), 1).astype(F32), 1.0, 0.0)
+            scale_all = lax.dot_general(
+                atom_hot, scales, NT, precision=lax.Precision.HIGHEST, preferred_element_type=F32
+            )
+            own_slot = iota((terms, slots), 1).astype(F32) == slot_col
+            scale_row = as_row(jnp.sum(jnp.where(own_slot, scale_all, 0.0), axis=1, keepdims=True))
+
+            shared = mm(jnp.ones((16, face_pad), BF16), face_spot[:, 0:face_pad], NT)[0:1]
+            roots[...] = jnp.zeros(roots.shape, F32)
+            roots[:, :nodes] = jnp.sqrt(mass[...])
+            weight_row = (1.0 - shared) * roots[...]
+            roots[...] = weight_row
 
         gathered = mm(values, spots[...], NN).astype(BF16)
         for c in range(cells):
@@ -269,12 +276,7 @@
         held_ref[...] = assembled + lead * arrived
         current = held_ref[...]
 
-    filtered[...] = current[:, :nodes]
-    shared = mm(jnp.ones((16, face_pad), BF16), face_spot[:, 0:face_pad], NT)[0:1]
-    y0[...] = jnp.zeros(y0.shape, F32)
-    y0[0:1, :nodes] = jnp.sqrt(mass[...])
-    weight = (1.0 - shared) * y0[0:1, :]
-    zed = (current * weight).astype(BF16)
+    zed = (current * roots[...]).astype(BF16)
     half = zed_half.shape[2]
     zed_half[0] = zed[:, :half]
     zed_half[1] = zed[:, half:]
@@ -288,6 +290,7 @@
         )
         copy.start()
         copies.append(copy)
+    filtered[...] = current[:, :nodes]
     own_block = mm(zed, zed, NT)
     for copy in copies:
         copy.wait_recv()
@@ -371,6 +374,7 @@
             pltpu.VMEM((bands, node_pad), F32),
             pltpu.VMEM((bands, node_pad), F32),
             pltpu.VMEM((bands, node_pad), F32),
+            pltpu.VMEM((1, node_pad), F32),
             pltpu.VMEM((8, terms), F32),
             pltpu.VMEM((peers, 8, terms), F32),
             pltpu.VMEM((3, bands, terms), F32),
@@ -399,7 +403,7 @@
         share_list.reshape(share_list.shape[1:]),
         contacts,
         proj_values,
-        coupling,
+        coupling.T,
         proj_count.reshape(1, -1),
         mass.reshape(1, -1),
     )

time: 57 us -> 54.6 us (0.958)
  Pallas kernels: 51.4 us -> 49.8 us
  local copies, waits for them, and re-layouts: 4.61 us -> 3.87 us
    pallas_call x1, Pallas kernels: 51.4 us -> 49.8 us  [on_device(): pl.pallas_call(functools.partial(kernel, n_cell, n_band), out_shape=(jax....]
    unnamed x16 -> x17, local copies, waits for them, and re-layouts: 3.91 us -> 3.17 us
where the time goes in v3:
time: 54.6 us; the launch traced here: 54.4 us
  Pallas kernels  49.8 us (91%)
  local copies, waits for them, and re-layouts  3.87 us (7%)
  between operations  0.74 us (1%)
    pallas_call x1, Pallas kernels, on_device(): pl.pallas_call(functools.partial(kernel, n_cell, n_band), out_shape=(jax....  49.8 us
    unnamed x17, local copies, waits for them, and re-layouts  3.17 us

profile of v3, /device:TPU:0, one launch (start us, length us, event | category | flops | bytes accessed | tf_op | source)
XLA Modules:
  0.0 54.4 jit_solution(132232013557506954)
XLA Ops:
  0.6 0.7 %reshape.15.mass = f32[1,1183]{1,0:T(1,128)S(1)} reshape(f32[1183]{0:T(1024)} %param.17) | data formatting | bytes 9464 | tf_op jit(solution)/shard_map/reshape | solution.py:408
  1.3 0.0 copy-start
  1.3 0.0 copy-start.1
  1.3 0.0 copy-start.2
  1.3 0.0 copy-start.3
  1.4 0.0 copy-start.4
  1.4 0.0 copy-start.5
  1.4 0.0 copy-start.6
  1.4 1.8 %copy.11.cell_matrix = f32[4,343,343]{2,1,0:T(8,128)S(1)} copy(f32[4,343,343]{2,0,1:T(4,128)} %param.10) | data formatting | bytes 3764768 | tf_op args[1]
  3.2 0.0 copy-done
  3.2 0.0 copy-done.1
  3.2 0.0 copy-done.2
  3.2 0.0 copy-done.3
  3.3 0.0 copy-done.4
  3.3 0.0 copy-done.5
  3.3 0.0 copy-done.6
  3.3 49.8 %shard_map.104 = (f32[48,1183]{1,0:T(8,128)S(1)}, f32[48,192]{1,0:T(8,128)S(1)}) custom-call(f32[48,1183]{1,0:T(8,128)S(1)} %copy-done, f32[4,343,343]{2,1,0:T(8,128)S(1)} %copy.11.cell_matrix, s32[4,343]{1,0:T(4,128)S(1)} %copy-done.2, s32[2,169]{1,0:T(2,128)S(1)} %bitcast.4, s32[2,16]{1,0:T(2,128)S(1)} %copy-done.5, f32[16,8,343]{2,1,0:T(8,128)S(1)} %copy-done.1, ...), custom_call_target="tpu_custom_call" | custom-call | tf_op jit(solution)/shard_map/pallas_call | solution.py:355
  53.1 0.7 %copy.14 = f32[48,1183]{1,0:T(8,128)} copy(f32[48,1183]{1,0:T(8,128)S(1)} %get-tuple-element.4) | data formatting | bytes 454272
  53.8 0.6 %copy.15 = f32[48,192]{1,0:T(8,128)} copy(f32[48,192]{1,0:T(8,128)S(1)} %get-tuple-element.5) | data formatting | bytes 73728
Async XLA Ops:
  1.3 1.9 %copy-start = (f32[48,1183]{1,0:T(8,128)S(1)}, f32[48,1183]{1,0:T(8,128)}, u32[]{:S(2)}) copy-start(f32[48,1183]{1,0:T(8,128)} %waves.1) | copy-start | bytes 681412
  1.3 1.9 %copy-start.1 = (f32[16,8,343]{2,1,0:T(8,128)S(1)}, f32[16,8,343]{2,1,0:T(8,128)}, u32[]{:S(2)}) copy-start(f32[16,8,343]{2,1,0:T(8,128)} %proj_values.1) | copy-start | bytes 526852
  1.3 1.9 %copy-start.2 = (s32[4,343]{1,0:T(4,128)S(1)}, s32[4,343]{1,0:T(4,128)}, u32[]{:S(2)}) copy-start(s32[4,343]{1,0:T(4,128)} %node_map.1) | copy-start | bytes 16468
  1.3 1.9 %copy-start.3 = (f32[32,8]{0,1:T(8,128)S(1)}, f32[32,8]{0,1:T(8,128)}, u32[]{:S(2)}) copy-start(f32[32,8]{0,1:T(8,128)} %param.15) | copy-start | bytes 3076
  1.4 1.9 %copy-start.4 = (s32[1,2,169]{2,1,0:T(2,128)S(1)}, s32[1,2,169]{2,1,0:T(2,128)}, u32[]{:S(2)}) copy-start(s32[1,2,169]{2,1,0:T(2,128)} %param.12) | copy-start | bytes 4060
  1.4 1.9 %copy-start.5 = (s32[2,16]{1,0:T(2,128)S(1)}, s32[2,16]{1,0:T(2,128)}, u32[]{:S(2)}) copy-start(s32[2,16]{1,0:T(2,128)} %contacts.1) | copy-start | bytes 388
  1.4 1.9 %copy-start.6 = (s32[32]{0:T(128)S(1)}, s32[32]{0:T(128)}, u32[]{:S(2)}) copy-start(s32[32]{0:T(128)} %param.16) | copy-start | bytes 388
